TPU v7x, 512 devices: a whole 4x8x8 slice. The times are simulated.
512 devices in a mesh: tile: 16 (over y, x_lo), date: 32 (over z, x_hi, core).
Axes of the slice: x: 4 (x_hi: 2, x_lo: 2; x = x_hi * 2 + x_lo), y: 8, z: 8, core: 2. Of those that a mesh axis runs over, the one named last changes fastest.
Arguments:
- primary: bfloat16 [32, 16, 4096], P('tile', None, 'date'), parts along dimension 0, may hold values from -6 to 6
- secondaries: bfloat16 [64, 32, 32, 4224], P('date', 'tile'), parts along dimension 1, may hold values from -6 to 6
- shift_az: int32 [1024], P(('tile', 'date')), parts along dimension 0, may hold values from 0 to 8
- shift_rg: int32 [1024], P(('tile', 'date')), parts along dimension 0, may hold values from 0 to 120
- frac_index: int32 [64, 32], P('date', 'tile'), parts along dimension 1, may hold values from 0 to 63
Outputs:
- filtered: float32 [32, 64, 1024], P('tile', None, 'date'), parts along dimension 0
There are 16 independent parts, one for each index of `tile`. A program takes and returns all parts, laid end to end along the dimension named above; each array names one. Nothing has to cross between parts.
All inputs are finite; a program needn't handle non-finite values.
Results may differ from a plain program's by a relative error of at most 0.0028.
Values may be sent and summed in bfloat16 or wider, within the bound.
A program may use at most 64 MiB of HBM per device.

v0:
```python
import jax
import jax.numpy as jnp
from jax import lax
from jax.sharding import PartitionSpec as P

AZ = 16
RG = 4096
FRAC = 64
LOOK_AZ = 4
LOOK_RG = 16


def sinc_taps(index):
    frac = index.astype(jnp.float32) / FRAC
    t = jnp.arange(8, dtype=jnp.float32) - 3.0 - frac
    return jnp.sinc(t) * (0.5 + 0.5 * jnp.cos(jnp.pi * t / 4.0))


def resample(args):
    slab, off_az, off_rg, fracs = args
    taps_az = sinc_taps(fracs[0])
    taps_rg = sinc_taps(fracs[1])
    width = slab.shape[2]
    along = jnp.zeros((2, AZ, width), jnp.float32)
    for i in range(8):
        piece = lax.dynamic_slice(slab, (jnp.int32(0), off_az + i, jnp.int32(0)), (2, AZ, width))
        along = along + taps_az[i] * piece.astype(jnp.float32)
    result = jnp.zeros((2, AZ, RG), jnp.float32)
    for j in range(8):
        piece = lax.dynamic_slice(along, (jnp.int32(0), jnp.int32(0), off_rg + j), (2, AZ, RG))
        result = result + taps_rg[j] * piece
    return result.astype(jnp.bfloat16)


def box_mean(values):
    lead = values.shape[:-2]
    lines, samples = values.shape[-2:]
    shaped = values.reshape(lead + (lines // LOOK_AZ, LOOK_AZ, samples // LOOK_RG, LOOK_RG))
    return shaped.mean(axis=(-3, -1))


def looks_of(done, prim):
    sec_re = done[:, 0].astype(jnp.float32)
    sec_im = done[:, 1].astype(jnp.float32)
    prim_re = prim[0].astype(jnp.float32)[None]
    prim_im = prim[1].astype(jnp.float32)[None]
    ifg_re = sec_re * prim_re + sec_im * prim_im
    ifg_im = sec_im * prim_re - sec_re * prim_im
    return (box_mean(ifg_re), box_mean(ifg_im), box_mean(sec_re * sec_re + sec_im * sec_im))


def normalize(sum_re, sum_im, power_sec, prim):
    prim_f = prim.astype(jnp.float32)
    power_prim = box_mean(prim_f[0] * prim_f[0] + prim_f[1] * prim_f[1])
    scale = jnp.sqrt(float(LOOK_AZ * LOOK_RG)) / jnp.sqrt(
        (power_prim[None] + 1e-06) * (power_sec + 1e-06)
    )
    return (sum_re * scale, sum_im * scale)


def shards(primary, secondaries, shift_az, shift_rg, frac_index):
    gathered = lax.all_gather(primary, "date", axis=2, tiled=True)
    resampled = lax.map(resample, (secondaries, shift_az, shift_rg, frac_index))
    count = lax.axis_size("date")
    mine = lax.axis_index("date")
    columns = RG // count
    prim_cols = lax.dynamic_slice_in_dim(gathered, mine * columns, columns, 2)
    local_re, local_im, local_pow = looks_of(resampled, gathered)
    sum_re, sum_im, power_sec = (
        lax.all_to_all(local_re, "date", split_axis=2, concat_axis=0, tiled=True),
        lax.all_to_all(local_im, "date", split_axis=2, concat_axis=0, tiled=True),
        lax.all_to_all(local_pow, "date", split_axis=2, concat_axis=0, tiled=True),
    )
    norm_re, norm_im = normalize(sum_re, sum_im, power_sec, prim_cols)
    dates = norm_re.shape[0]
    coh_re = jnp.transpose(norm_re, (0, 2, 1)).reshape(dates, -1)
    coh_im = jnp.transpose(norm_im, (0, 2, 1)).reshape(dates, -1)
    spread = dates / 8.0
    order = jnp.arange(dates, dtype=jnp.float32)
    weights = jnp.exp(-((order[:, None] - order[None, :]) ** 2) / (2.0 * spread * spread))
    weights = weights / jnp.sum(weights, axis=1, keepdims=True)
    out_re = coh_re - jnp.dot(weights, coh_re, precision=lax.Precision.HIGHEST)
    out_im = coh_im - jnp.dot(weights, coh_im, precision=lax.Precision.HIGHEST)
    return jnp.stack([out_re, out_im])


def solution(mesh):
    in_specs = (
        P("tile", None, "date"),
        P("date", "tile", None, None),
        P(("tile", "date")),
        P(("tile", "date")),
        P("date", "tile"),
    )
    out_specs = P("tile", None, "date")
    return jax.shard_map(shards, mesh=mesh, in_specs=in_specs, out_specs=out_specs, check_vma=False)
```

profile of v0, /device:TPU:1, one launch (start us, length us, event | category | flops | bytes accessed | tf_op | source)
XLA Modules:
  0.0 203.1 jit_solution(4117676593541596732)
XLA Ops:
  0.0 85.4 %while.13 = (s32[]{:T(128)}, bf16[2,2,16,4096]{3,2,1,0:T(8,128)(2,1)S(1)}, s32[2,2]{1,0:T(2,128)}, s32[2]{0:T(128)}, bf16[2,2,32,4224]{3,2,1,0:T(8,128)(2,1)}, /...) while((s32[]{:T(128)}, ...), condition=%wide.region_1.3_spmd, body=%wide.region_0.2_spmd.sunk | while | flops 5206717 | bytes 7161385 | solution.py:63
  0.0 1.3 dynamic_slice.143
  2.5 0.7 constant_dynamic-slice_fusion.2
  3.2 0.6 fusion.34
  4.5 0.7 fusion.36
  14.7 8.3 %add_add_fusion.2 = f32[1,2,16,4224]{3,2,1,0:T(8,128)S(1)} fusion(bf16[2,2,32,4224]{3,2,1,0:T(8,128)(2,1)} %get-tuple-element.347, s32[]{:T(128)S(6)} %dynamic_slice.142, s32[]{:T(128)S(6)} %select_n.243, f32[]{:T(128)} %bitcast.84, s32[]{:T(128)S(6)} %select_n.245, f32[]{:T(128)} %bitcast.85, s32[]{:T(128)S(6)} %select_n.247, f32[]{:T(128)} %bitcast.86, ...), kind=kLoop, calls=%fused_computation.clone.1 | loop fusion | flops 3108864 | bytes 2703428 | tf_op jit(solution)/shard_map/while/body/eval_jaxpr/add | solution.py:27
  23.1 1.3 dynamic_slice.144
  26.2 0.7 fusion.38
  36.5 6.1 %bitcast_dynamic-update-slice_fusion.2 = bf16[2,2,16,4096]{3,2,1,0:T(8,128)(2,1)S(1)} fusion(bf16[2,2,16,4096]{3,2,1,0:T(8,128)(2,1)S(1)} %get-tuple-element.312, s32[]{:T(128)S(6)} %copy.57, f32[1,2,16,4224]{3,2,1,0:T(8,128)S(1)} %add_add_fusion.2, s32[]{:T(128)S(6)} %select_n.258, f32[]{:T(128)} %bitcast.94, s32[]{:T(128)S(6)} %select_n.259, ...), kind=kLoop, calls=%fused_computation.3.clone.1 | loop fusion | flops 2097152 | bytes 4456516 | tf_op jit(solution)/shard_map/while/body/jit(dynamic_update_index_in_dim)/dynamic_update_slice | solution.py:63
  42.6 1.3 dynamic_slice.143
  45.1 0.7 constant_dynamic-slice_fusion.2
  47.1 0.7 fusion.36
  57.3 8.7 %add_add_fusion.2 = f32[1,2,16,4224]{3,2,1,0:T(8,128)S(1)} fusion(bf16[2,2,32,4224]{3,2,1,0:T(8,128)(2,1)} %get-tuple-element.347, s32[]{:T(128)S(6)} %dynamic_slice.142, s32[]{:T(128)S(6)} %select_n.243, f32[]{:T(128)} %bitcast.84, s32[]{:T(128)S(6)} %select_n.245, f32[]{:T(128)} %bitcast.85, s32[]{:T(128)S(6)} %select_n.247, f32[]{:T(128)} %bitcast.86, ...), kind=kLoop, calls=%fused_computation.clone.1 | loop fusion | flops 3108864 | bytes 2703428 | tf_op jit(solution)/shard_map/while/body/eval_jaxpr/add | solution.py:27
  66.0 1.3 dynamic_slice.144
  69.2 0.7 fusion.38
  79.4 6.1 %bitcast_dynamic-update-slice_fusion.2 = bf16[2,2,16,4096]{3,2,1,0:T(8,128)(2,1)S(1)} fusion(bf16[2,2,16,4096]{3,2,1,0:T(8,128)(2,1)S(1)} %get-tuple-element.312, s32[]{:T(128)S(6)} %copy.57, f32[1,2,16,4224]{3,2,1,0:T(8,128)S(1)} %add_add_fusion.2, s32[]{:T(128)S(6)} %select_n.258, f32[]{:T(128)} %bitcast.94, s32[]{:T(128)S(6)} %select_n.259, ...), kind=kLoop, calls=%fused_computation.3.clone.1 | loop fusion | flops 2097152 | bytes 4456516 | tf_op jit(solution)/shard_map/while/body/jit(dynamic_update_index_in_dim)/dynamic_update_slice | solution.py:63
  85.5 2.8 %reshape.142 = f32[2,4,4,256,16]{4,3,2,1,0:T(8,128)} reshape(f32[2,1,16,4096]{3,2,1,0:T(8,128)S(1)} %get-tuple-element.201) | data formatting | bytes 1048576 | tf_op jit(solution)/shard_map/convert_element_type | solution.py:44
  88.3 2.8 %reshape.140 = f32[2,4,4,256,16]{4,3,2,1,0:T(8,128)} reshape(f32[2,1,16,4096]{3,2,1,0:T(8,128)S(1)} %get-tuple-element.200) | data formatting | bytes 1048576 | tf_op jit(solution)/shard_map/convert_element_type | solution.py:43
  91.1 49.9 %all_gather.3 = bf16[2,16,4096]{2,1,0:T(8,128)(2,1)S(1)} all-gather(bf16[2,16,128]{2,1,0:T(8,128)(2,1)S(1)} %copy-done), channel_id=1, replica_groups=mesh['tile'=16,'date'=32] {'date'}, dimensions={2}, use_global_device_ids=true | all-gather | bytes 270336 | tf_op jit(solution)/shard_map/all_gather | solution.py:62
  141.1 0.7 reshape.143
  141.8 2.1 %reshape.141 = f32[4,4,256,16]{3,2,1,0:T(8,128)} reshape(f32[1,16,4096]{2,1,0:T(8,128)S(1)} %get-tuple-element.202) | data formatting | bytes 524288 | tf_op jit(solution)/shard_map/mul | solution.py:47
  143.9 5.4 %add_reduce_fusion.1 = (f32[2,4,256]{2,1,0:T(4,128)S(1)}, f32[2,4,256]{2,1,0:T(4,128)S(1)}, f32[2,4,256]{2,1,0:T(4,128)S(1)}) fusion(f32[2,4,4,256,16]{4,3,2,1,0:T(8,128)} %reshape.142, f32[2,4,4,256,16]{4,3,2,1,0:T(8,128)} %reshape.140, f32[4,4,256,16]{3,2,1,0:T(8,128)S(1)} %reshape.143, f32[4,4,256,16]{3,2,1,0:T(8,128)} %reshape.141), kind=kLoop, calls=%fused_computation.36 | loop fusion | flops 1566720 | bytes 1597440 | tf_op jit(solution)/shard_map/reduce_sum | solution.py:39
  149.4 0.9 copy.44
  150.2 3.7 %all-to-all-start.1 = ((f32[2,4,256]{1,0,2:T(2,128)}), f32[2,4,256]{1,0,2:T(2,128)S(1)}, u32[]{:S(2)}, u32[]{:S(2)}) async-start(f32[2,4,256]{1,0,2:T(2,128)} %copy.44), calls=%async_computation.1 | async-start | bytes 524288 | tf_op jit(solution)/shard_map/all_to_all | solution.py:72
  154.0 0.9 copy.41
  155.0 11.9 %all-to-all-done.1 = f32[2,4,256]{1,0,2:T(2,128)S(1)} async-done(((f32[2,4,256]{1,0,2:T(2,128)}), f32[2,4,256]{1,0,2:T(2,128)S(1)}, u32[]{:S(2)}, u32[]{:S(2)}) %all-to-all-start.1) | async-done | bytes 8224 | tf_op jit(solution)/shard_map/all_to_all | solution.py:72
  166.9 4.2 %all-to-all-start = ((f32[2,4,256]{1,0,2:T(2,128)}), f32[2,4,256]{1,0,2:T(2,128)S(1)}, u32[]{:S(2)}, u32[]{:S(2)}) async-start(f32[2,4,256]{1,0,2:T(2,128)} %copy.41), calls=%async_computation | async-start | bytes 524288 | tf_op jit(solution)/shard_map/all_to_all | solution.py:70
  171.1 0.9 copy.48
  172.2 11.8 %all-to-all-done = f32[2,4,256]{1,0,2:T(2,128)S(1)} async-done(((f32[2,4,256]{1,0,2:T(2,128)}), f32[2,4,256]{1,0,2:T(2,128)S(1)}, u32[]{:S(2)}, u32[]{:S(2)}) %all-to-all-start) | async-done | bytes 8224 | tf_op jit(solution)/shard_map/all_to_all | solution.py:70
  184.0 4.1 %all-to-all-start.2 = ((f32[2,4,256]{1,0,2:T(2,128)}), f32[2,4,256]{1,0,2:T(2,128)S(1)}, u32[]{:S(2)}, u32[]{:S(2)}) async-start(f32[2,4,256]{1,0,2:T(2,128)} %copy.48), calls=%async_computation.2 | async-start | bytes 524288 | tf_op jit(solution)/shard_map/all_to_all | solution.py:71
  189.1 12.1 %all-to-all-done.2 = f32[2,4,256]{1,0,2:T(2,128)S(1)} async-done(((f32[2,4,256]{1,0,2:T(2,128)}), f32[2,4,256]{1,0,2:T(2,128)S(1)}, u32[]{:S(2)}, u32[]{:S(2)}) %all-to-all-start.2) | async-done | bytes 8224 | tf_op jit(solution)/shard_map/all_to_all | solution.py:71
  202.5 0.6 pad_maximum_fusion
  (32 shorter events, 3.5 us)
Async XLA Ops:
  85.5 5.6 %copy-start = (bf16[2,16,128]{2,1,0:T(8,128)(2,1)S(1)}, bf16[2,16,128]{2,1,0:T(8,128)(2,1)}, u32[]{:S(2)}) copy-start(bf16[2,16,128]{2,1,0:T(8,128)(2,1)} %param.8) | copy-start | bytes 24580
  150.2 16.7 %all-to-all-start.1 = ((f32[2,4,256]{1,0,2:T(2,128)}), f32[2,4,256]{1,0,2:T(2,128)S(1)}, u32[]{:S(2)}, u32[]{:S(2)}) async-start(f32[2,4,256]{1,0,2:T(2,128)} %copy.44), calls=%async_computation.1 | async-start | bytes 524288 | tf_op jit(solution)/shard_map/all_to_all | solution.py:72
  166.9 17.2 %all-to-all-start = ((f32[2,4,256]{1,0,2:T(2,128)}), f32[2,4,256]{1,0,2:T(2,128)S(1)}, u32[]{:S(2)}, u32[]{:S(2)}) async-start(f32[2,4,256]{1,0,2:T(2,128)} %copy.41), calls=%async_computation | async-start | bytes 524288 | tf_op jit(solution)/shard_map/all_to_all | solution.py:70
  184.0 17.1 %all-to-all-start.2 = ((f32[2,4,256]{1,0,2:T(2,128)}), f32[2,4,256]{1,0,2:T(2,128)S(1)}, u32[]{:S(2)}, u32[]{:S(2)}) async-start(f32[2,4,256]{1,0,2:T(2,128)} %copy.48), calls=%async_computation.2 | async-start | bytes 524288 | tf_op jit(solution)/shard_map/all_to_all | solution.py:71
where the time goes:
time: 204 us; the launch traced here: 203 us
  blocking collectives  49.9 us (24%)
  loops' own time  45.7 us (22%)
  other arithmetic  35.8 us (18%)
  waiting for transfers between devices  35.8 us (18%)
  local copies, waits for them, and re-layouts  23.1 us (11%)
  starting transfers between devices  12 us (6%)
    all_gather x1, blocking collectives, shards(): gathered = lax.all_gather(primary, 'date', axis=2, tiled=True)  49.9 us
    another operation x1, loops' own time, shards(): resampled = lax.map(resample, (secondaries, shift_az, shift_rg, frac_index))  45.7 us
    add x2, other arithmetic, resample(): along = along + taps_az[i] * piece.astype(jnp.float32)  17 us
    dynamic_update_slice x2, other arithmetic, shards(): resampled = lax.map(resample, (secondaries, shift_az, shift_rg, frac_index))  12.1 us
    all_to_all x1, waiting for transfers between devices, shards(): lax.all_to_all(local_im, 'date', split_axis=2, concat_axis=0, tiled=True)  12.1 us
    all_to_all x1, waiting for transfers between devices, shards(): lax.all_to_all(local_pow, 'date', split_axis=2, concat_axis=0, tiled=True)  11.9 us
    all_to_all x1, waiting for transfers between devices, shards(): lax.all_to_all(local_re, 'date', split_axis=2, concat_axis=0, tiled=True)  11.8 us
    dynamic_slice x6, local copies, waits for them, and re-layouts, shards(): resampled = lax.map(resample, (secondaries, shift_az, shift_rg, frac_index))  6.45 us
  transfers between devices with their start and end apart: 3, of which 3 were waited for; matrix products, arithmetic and copies ran while one was open for 1% of the time, Pallas kernels for 0%

commit v1 on v0

v1 whole, which is shorter than its diff:
```python
import functools

import jax
import jax.numpy as jnp
from jax import lax
from jax.experimental import pallas as pl
from jax.experimental.pallas import tpu as pltpu
from jax.sharding import PartitionSpec as P

F32 = jnp.float32
BF16 = jnp.bfloat16
AZ = 16
RG = 4096
WIDTH = 4224
BLOCK = 128
NB = RG // BLOCK
MESH = pl.DeviceIdType.MESH


def iota(shape, dim):
    return lax.broadcasted_iota(jnp.int32, shape, dim)


def split(x):
    hi = x.astype(BF16)
    return hi, (x - hi.astype(F32)).astype(BF16)


def dot(a, b):
    return jnp.dot(a, b, preferred_element_type=F32)


def taps_of(index):
    i = iota((8, 128), 0)
    t = i.astype(F32) - 3.0 - index.astype(F32) / 64.0
    pt = jnp.pi * t
    sinc = jnp.where(t == 0.0, 1.0, jnp.sin(pt) / jnp.where(t == 0.0, 1.0, pt))
    return sinc * (0.5 + 0.5 * jnp.cos(pt / 4.0))


def azimuth_matrix(a, taps):
    row, col = iota((64, 128), 0), iota((64, 128), 1)
    line = (row % 4) * 4 + (row // 8) % 4
    first = row < 32
    same = (row // 32 == col // 64) & ((row // 4) % 2 == (col // 32) % 2)
    u = col % 32 - line - jnp.where(first, a[0], a[1])
    out = jnp.zeros((64, 128), F32)
    for j in range(8):
        out = jnp.where(u == j, jnp.where(first, taps[0][j : j + 1], taps[1][j : j + 1]), out)
    return jnp.where(same, out, 0.0)


def range_matrix(r, taps):
    u = iota((256, 128), 0) - iota((256, 128), 1) - r
    out = jnp.zeros((256, 128), F32)
    for j in range(8):
        out = jnp.where(u == j, taps[j : j + 1], out)
    return out


def kernel(
    saz, srg, frac, prim_ref, sec_ref, out_ref,
    slab, along, perm, gath, msg, rx, slab_sem, psend, precv, msend, mrecv,
):
    n = NB
    me = lax.axis_index("date")
    chunks = 3
    cw = WIDTH // chunks

    def load(c):
        cols = pl.ds(c * cw, cw)
        return pltpu.make_async_copy(sec_ref.at[:, cols], slab.at[:, cols], slab_sem.at[c])

    for c in range(chunks):
        load(c).start()

    barrier = pltpu.get_barrier_semaphore()

    @pl.loop(1, n)
    def _(k):
        pl.semaphore_signal(barrier, inc=1, device_id={"date": lax.rem(me + k, n)}, device_id_type=MESH)

    row, col = iota((32, 32), 0), iota((32, 32), 1)
    want = ((row // 4) % 2) * 16 + (row % 4) * 4 + row // 8
    order = jnp.where(col == want, 1.0, 0.0).astype(BF16)
    mine = dot(order, prim_ref[...]).astype(BF16)
    perm[...] = mine
    gath[me] = mine

    pl.semaphore_wait(barrier, n - 1)

    def prim_copy(k, src, dst):
        return pltpu.make_async_remote_copy(
            src_ref=perm, dst_ref=gath.at[src], send_sem=psend.at[k], recv_sem=precv.at[src],
            device_id={"date": dst}, device_id_type=MESH,
        )

    @pl.loop(1, n)
    def _(k):
        prim_copy(k, me, lax.rem(me + k, n)).start()

    taps = [[taps_of(frac[d, x]) for x in range(2)] for d in range(2)]
    a_hi, a_lo = split(azimuth_matrix((saz[0], saz[1]), (taps[0][0], taps[1][0])))
    a_both = jnp.concatenate([a_hi, a_lo], axis=0)
    for c in range(chunks):
        load(c).wait()
        cols = pl.ds(c * cw, cw)
        y = dot(a_both, slab[:, cols])
        hi, lo = split(y[:64] + y[64:])
        for d in range(2):
            along[d, :32, cols] = hi[32 * d : 32 * d + 32]
            along[d, 32:, cols] = lo[32 * d : 32 * d + 32]

    res = []
    for d in range(2):
        b_hi, b_lo = split(range_matrix(srg[d], taps[d][1]))
        b_both = jnp.concatenate([b_hi, b_lo], axis=1)
        whole = along[d]
        rows = jnp.concatenate([whole[:, BLOCK * b : BLOCK * b + 256] for b in range(n)], axis=0)
        y = dot(rows, b_both).reshape(n, 64, 256)
        full = y[:, :32, :128] + (y[:, :32, 128:] + y[:, 32:, :128])
        res.append(full.astype(BF16).astype(F32).reshape(n, 4, 8, 128))

    @pl.loop(1, n)
    def _(k):
        src = lax.rem(me + n - k, n)
        prim_copy(k, src, src).wait_recv()

    p = gath[...].astype(F32).reshape(n, 4, 8, 128)
    swapped = jnp.concatenate([p[:, :, 4:], p[:, :, :4]], axis=2)
    kinds = []
    for d in range(2):
        kinds += [jnp.sum(res[d] * p, axis=1), jnp.sum(res[d] * swapped, axis=1)]
    kinds += [jnp.sum(res[d] * res[d], axis=1) for d in range(2)]
    kinds += [jnp.sum(p * p, axis=1)]
    x = jnp.stack(kinds, axis=1).reshape(n * 7 * 8, 128)
    x_hi, x_lo = split(x)
    x_both = jnp.concatenate([x_hi, x_lo], axis=1)
    look = (iota((256, 128), 0) % 128) // 16
    box = jnp.where(look == (iota((256, 128), 1) % 32) // 4, 1.0, 0.0).astype(BF16)
    y = dot(x_both, box).reshape(n, 7, 8, 128)
    sub, lane = iota((8, 128), 0), iota((8, 128), 1)
    hit = jnp.where(sub % 4 == lane % 4, 1.0 / 64.0, 0.0)
    flip = jnp.where(sub < 4, -hit, hit)
    of = lane // 32
    zero = jnp.zeros_like(hit)
    s = jnp.zeros((n, 8, 128), F32)
    for k in range(4):
        s = s + y[:, k] * jnp.where(of == k, flip if k % 2 else hit, zero)[None]
    q = y[:, 4] * jnp.where(of < 2, hit, zero)[None] + y[:, 5] * jnp.where(of < 2, zero, hit)[None]
    pw = y[:, 6] * hit[None]
    s, q, pw = jnp.sum(s, axis=1), jnp.sum(q, axis=1), jnp.sum(pw, axis=1)
    coherent = s * (8.0 / jnp.sqrt((pw + 1e-06) * (q + 1e-06)))
    msg[...] = coherent.reshape(n, 1, 128)
    rx[me] = msg[me]

    def msg_copy(k, src, dst):
        return pltpu.make_async_remote_copy(
            src_ref=msg.at[dst], dst_ref=rx.at[src], send_sem=msend.at[k], recv_sem=mrecv.at[src],
            device_id={"date": dst}, device_id_type=MESH,
        )

    @pl.loop(1, n)
    def _(k):
        msg_copy(k, me, lax.rem(me + k, n)).start()

    row, col = iota((64, 256), 0), iota((64, 256), 1)
    gap = (row - ((col % 32) * 2 + (col // 32) % 2)).astype(F32)
    w = jnp.exp(-(gap * gap) / 128.0)
    total = jnp.sum(jnp.where(col < 64, w, 0.0), axis=1, keepdims=True)
    high = jnp.where(gap == 0.0, 1.0, 0.0) - w / total
    h_hi, h_lo = split(high)
    filt = jnp.where((col // 64) % 2 == 0, h_hi.astype(F32), h_lo.astype(F32)).astype(BF16)

    @pl.loop(1, n)
    def _(k):
        src = lax.rem(me + n - k, n)
        msg_copy(k, src, src).wait_recv()

    c = rx[...].reshape(n, 128)
    c = jnp.concatenate([c, pltpu.roll(c, 64, 1)], axis=0)
    c_hi, c_lo = split(c)
    out = dot(filt, jnp.concatenate([c_hi, c_hi, c_lo, c_lo], axis=0)).T
    out_ref[0] = out[:32]
    out_ref[1] = out[32:64]

    @pl.loop(1, n)
    def _(k):
        dst = lax.rem(me + k, n)
        prim_copy(k, me, dst).wait_send()
        msg_copy(k, me, dst).wait_send()


def shards(primary, secondaries, shift_az, shift_rg, frac_index):
    n = NB
    vmem = pl.BlockSpec(memory_space=pltpu.VMEM)
    smem = pl.BlockSpec(memory_space=pltpu.SMEM)
    out = pl.pallas_call(
        kernel,
        out_shape=jax.ShapeDtypeStruct((2, 32, 64), F32),
        in_specs=[smem, smem, smem, vmem, pl.BlockSpec(memory_space=pltpu.HBM)],
        out_specs=vmem,
        scratch_shapes=[
            pltpu.VMEM((128, WIDTH), BF16),
            pltpu.VMEM((2, 64, WIDTH), BF16),
            pltpu.VMEM((32, 128), BF16),
            pltpu.VMEM((n, 32, 128), BF16),
            pltpu.VMEM((n, 1, 128), F32),
            pltpu.VMEM((n, 1, 128), F32),
            pltpu.SemaphoreType.DMA((3,)),
            pltpu.SemaphoreType.DMA((n,)),
            pltpu.SemaphoreType.DMA((n,)),
            pltpu.SemaphoreType.DMA((n,)),
            pltpu.SemaphoreType.DMA((n,)),
        ],
        compiler_params=pltpu.CompilerParams(
            collective_id=0, has_side_effects=True, vmem_limit_bytes=64 * 2**20
        ),
    )(shift_az, shift_rg, frac_index, primary.reshape(32, 128), secondaries.reshape(128, WIDTH))
    return jnp.transpose(out, (0, 2, 1))


def solution(mesh):
    in_specs = (
        P("tile", None, "date"),
        P("date", "tile", None, None),
        P(("tile", "date")),
        P(("tile", "date")),
        P("date", "tile"),
    )
    out_specs = P("tile", None, "date")
    return jax.shard_map(shards, mesh=mesh, in_specs=in_specs, out_specs=out_specs, check_vma=False)
```

time: 204 us -> 35.2 us (0.17)
  blocking collectives: 49.9 us -> 0 us
  loops' own time: 45.7 us -> 0 us
  other arithmetic: 35.8 us -> 0 us
  waiting for transfers between devices: 35.8 us -> 0 us
  Pallas kernels: 0 us -> 33.6 us
  local copies, waits for them, and re-layouts: 23.1 us -> 1.38 us
  starting transfers between devices: 12 us -> 0 us
    all_gather x1 -> x0, blocking collectives: 49.9 us -> none  [shards(): gathered = lax.all_gather(primary, 'date', axis=2, tiled=True)]
    another operation x1 -> x0, loops' own time: 45.7 us -> none  [shards(): resampled = lax.map(resample, (secondaries, shift_az, shift_rg, frac_index))]
    all_to_all x3 -> x0, waiting for transfers between devices: 35.8 us -> none  [the longest x1 12.1 us: shards(): lax.all_to_all(local_im, 'date', split_axis=2, concat_axis=0, tiled=True)]
    pallas_call x0 -> x1, Pallas kernels: none -> 33.6 us  [shards(): pl.pallas_call(kernel, out_shape=jax.ShapeDtypeStruct((2, 32, 64), F32),...]
    add x5 -> x0, other arithmetic: 17 us -> none  [the longest x2 17 us: resample(): along = along + taps_az[i] * piece.astype(jnp.float32)]
    dynamic_update_slice x2 -> x0, other arithmetic: 12.1 us -> none  [shards(): resampled = lax.map(resample, (secondaries, shift_az, shift_rg, frac_index))]
    all_to_all x3 -> x0, starting transfers between devices: 12 us -> none  [the longest x1 4.21 us: shards(): lax.all_to_all(local_re, 'date', split_axis=2, concat_axis=0, tiled=True)]
    dynamic_slice x6 -> x0, local copies, waits for them, and re-layouts: 6.45 us -> none  [shards(): resampled = lax.map(resample, (secondaries, shift_az, shift_rg, frac_index))]
  transfers between devices with their start and end apart: 3 -> 0, of which waited for: 3 -> 0; matrix products, arithmetic and copies ran while one was open for 1% -> 0% of each run, Pallas kernels for 0% -> 0%
where the time goes in v1:
time: 35.2 us; the launch traced here: 35 us
  Pallas kernels  33.6 us (95%)
  local copies, waits for them, and re-layouts  1.38 us (4%)
    pallas_call x1, Pallas kernels, shards(): pl.pallas_call(kernel, out_shape=jax.ShapeDtypeStruct((2, 32, 64), F32),...  33.6 us
    unnamed x1, local copies, waits for them, and re-layouts  1.38 us

profile of v1, /device:TPU:1, one launch (start us, length us, event | category | flops | bytes accessed | tf_op | source)
XLA Modules:
  0.0 35.0 jit_solution(4350627128960050269)
XLA Ops:
  0.0 33.6 %shard_map.55 = f32[2,32,64]{2,1,0:T(8,128)} custom-call(s32[2]{0:T(128)} %saz.1, s32[2]{0:T(128)} %srg.1, s32[2,2]{1,0:T(2,128)} %frac.1, bf16[32,128]{1,0:T(8,128)(2,1)} %bitcast.5, bf16[128,4224]{1,0:T(8,128)(2,1)} %bitcast.3), custom_call_target="tpu_custom_call" | custom-call | tf_op jit(solution)/shard_map/pallas_call | solution.py:198
  33.6 1.4 %copy.7 = f32[2,64,32]{1,2,0:T(8,128)} copy(f32[2,64,32]{1,2,0:T(8,128)} %bitcast.4) | data formatting | bytes 32768

commit v2 on v1

v2 whole, which is shorter than its diff:
```python
import jax
import jax.numpy as jnp
from jax import lax
from jax.experimental import pallas as pl
from jax.experimental.pallas import tpu as pltpu
from jax.sharding import PartitionSpec as P

F32 = jnp.float32
BF16 = jnp.bfloat16
WIDTH = 4224
BLOCK = 128
NB = 32
HALF = NB // 2
PIECES = (0, 9, 17, 25, 33)
MESH = pl.DeviceIdType.MESH


def iota(shape, dim):
    return lax.broadcasted_iota(jnp.int32, shape, dim)


def split(x):
    hi = x.astype(BF16)
    return hi, (x - hi.astype(F32)).astype(BF16)


def dot(a, b):
    return jnp.dot(a, b, preferred_element_type=F32)


def taps_of(index):
    i = iota((8, 128), 0)
    t = i.astype(F32) - 3.0 - index.astype(F32) / 64.0
    pt = jnp.pi * t
    sinc = jnp.where(t == 0.0, 1.0, jnp.sin(pt) / jnp.where(t == 0.0, 1.0, pt))
    return sinc * (0.5 + 0.5 * jnp.cos(pt / 4.0))


def azimuth_matrix(a, taps):
    row, col = iota((64, 128), 0), iota((64, 128), 1)
    line = (row % 4) * 4 + (row // 8) % 4
    first = row < 32
    same = (row // 32 == col // 64) & ((row // 4) % 2 == (col // 32) % 2)
    u = col % 32 - line - jnp.where(first, a[0], a[1])
    out = jnp.zeros((64, 128), F32)
    for j in range(8):
        out = jnp.where(u == j, jnp.where(first, taps[0][j : j + 1], taps[1][j : j + 1]), out)
    return jnp.where(same, out, 0.0)


def range_matrix(r, taps):
    u = iota((256, 128), 0) - iota((256, 128), 1) - r
    out = jnp.zeros((256, 128), F32)
    for j in range(8):
        out = jnp.where(u == j, taps[j : j + 1], out)
    return out


def kernel(
    saz_ref, srg_ref, frac_ref, prim_ref, sec_ref, out_ref,
    saz, srg, frac, prim, slab, along, tx, rx, in_sem, send_sem, recv_sem, late_sem, go_sem,
):
    n = NB
    me = lax.axis_index("date")
    early = me < HALF

    small = [
        pltpu.make_async_copy(src, dst, in_sem.at[k])
        for k, (src, dst) in enumerate(((saz_ref, saz), (srg_ref, srg), (frac_ref, frac), (prim_ref, prim)))
    ]

    def piece(c):
        return pl.ds(PIECES[c] * BLOCK, (PIECES[c + 1] - PIECES[c]) * BLOCK)

    def load(c):
        return pltpu.make_async_copy(sec_ref.at[:, piece(c)], slab.at[:, piece(c)], in_sem.at[4 + c])

    for copy in small:
        copy.start()
    for c in range(4):
        load(c).start()

    barrier = pltpu.get_barrier_semaphore()

    @pl.when(early)
    def _():
        @pl.loop(0, n)
        def _(k):
            @pl.when(k != me)
            def _():
                pl.semaphore_signal(barrier, inc=1, device_id={"date": k}, device_id_type=MESH)

    for copy in small[:3]:
        copy.wait()
    taps = [[taps_of(frac[d, x]) for x in range(2)] for d in range(2)]
    a_hi, a_lo = split(azimuth_matrix((saz[0], saz[1]), (taps[0][0], taps[1][0])))
    a_both = jnp.concatenate([a_hi, a_lo], axis=0)
    b_both = []
    for d in range(2):
        b_hi, b_lo = split(range_matrix(srg[d], taps[d][1]))
        b_both.append(jnp.concatenate([b_hi, b_lo], axis=1))

    def resample(c):
        load(c).wait()
        y = dot(a_both, slab[:, piece(c)])
        hi, lo = split(y[:64] + y[64:])
        for d in range(2):
            along[d, :32, piece(c)] = hi[32 * d : 32 * d + 32]
            along[d, 32:, piece(c)] = lo[32 * d : 32 * d + 32]
        first = 8 * c
        for d in range(2):
            whole = along[d, :, pl.ds(first * BLOCK, 9 * BLOCK)]
            rows = jnp.concatenate([whole[:, BLOCK * b : BLOCK * b + 256] for b in range(8)], axis=0)
            y = dot(rows, b_both[d]).reshape(8, 64, 256)
            full = y[:, :32, :128] + (y[:, :32, 128:] + y[:, 32:, :128])
            tx[pl.ds(first, 8), pl.ds(32 * d, 32)] = full.astype(BF16)

    def block_copy(src, dst):
        return pltpu.make_async_remote_copy(
            src_ref=tx.at[dst], dst_ref=rx.at[src], send_sem=send_sem.at[dst], recv_sem=recv_sem.at[src],
            device_id={"date": dst}, device_id_type=MESH,
        )

    def send(lo, hi):
        @pl.loop(lo, hi)
        def _(k):
            @pl.when(k != me)
            def _():
                block_copy(me, k).start()

    resample(0)

    @pl.when(early)
    def _():
        pl.semaphore_wait(barrier, HALF - 1)

    @pl.when(jnp.logical_not(early))
    def _():
        pl.semaphore_wait(barrier, HALF)

        @pl.loop(0, HALF)
        def _(k):
            pl.semaphore_signal(late_sem.at[me // 4 - 4], inc=1, device_id={"date": k}, device_id_type=MESH)

    send(0, 8)
    resample(1)
    send(8, 16)
    resample(2)
    resample(3)

    @pl.when(early)
    def _():
        @pl.loop(0, 4)
        def _(j):
            plane = (me // 4 + 1 + j) % 4
            pl.semaphore_wait(late_sem.at[plane], 4)
            send(HALF + 4 * plane, HALF + 4 * plane + 4)

        @pl.when((me < 4) | (me >= 12))
        def _():
            first = HALF + me % 4 + 8 * (1 - me // 12)
            pl.semaphore_signal(go_sem, inc=1, device_id={"date": first}, device_id_type=MESH)
            pl.semaphore_signal(go_sem, inc=1, device_id={"date": first + 4}, device_id_type=MESH)

    @pl.when(jnp.logical_not(early))
    def _():
        pl.semaphore_wait(go_sem, 1)
        send(HALF, n)

    rx[me] = tx[me]

    small[3].wait()
    row, col = iota((32, 32), 0), iota((32, 32), 1)
    want = ((row // 4) % 2) * 16 + (row % 4) * 4 + row // 8
    order = jnp.where(col == want, 1.0, 0.0).astype(BF16)
    p = dot(order, prim[...]).reshape(4, 8, 128)
    swapped = jnp.concatenate([p[:, 4:], p[:, :4]], axis=1)

    look = (iota((256, 128), 0) % 128) // 16
    box = jnp.where(look == (iota((256, 128), 1) % 32) // 4, 1.0, 0.0).astype(BF16)
    sub, lane = iota((8, 128), 0), iota((8, 128), 1)
    hit = jnp.where(sub % 4 == lane % 4, 1.0 / 64.0, 0.0)
    part = lane // 32
    masks = (
        jnp.where(part == 0, hit, 0.0),
        jnp.where(part == 1, jnp.where(sub < 4, -hit, hit), 0.0),
        jnp.where(part >= 2, hit, 0.0),
    )

    def boxes(x):
        hi, lo = split(x)
        return dot(jnp.concatenate([hi, lo], axis=1), box)

    power = jnp.sum(boxes(jnp.sum(p * p, axis=0)) * hit, axis=0, keepdims=True)

    row, col = iota((64, 256), 0), iota((64, 256), 1)
    gap = (row - col % 64).astype(F32)
    w = jnp.exp(-(gap * gap) / 128.0)
    total = jnp.sum(jnp.where(col < 64, w, 0.0), axis=1, keepdims=True)
    high = jnp.where(gap == 0.0, 1.0, 0.0) - w / total
    h_hi, h_lo = split(high)
    filt = jnp.where((col // 64) % 2 == 0, h_hi.astype(F32), h_lo.astype(F32)).astype(BF16)

    means = []
    for lo, hi in ((0, 16), (16, 24), (24, 32)):
        count = 2 * (hi - lo)

        @pl.loop(lo, hi)
        def _(k):
            @pl.when(k != me)
            def _():
                block_copy(k, k).wait_recv()

        s = rx[lo:hi].astype(F32).reshape(count, 4, 8, 128)
        kinds = [jnp.sum(s * p[None], axis=1), jnp.sum(s * swapped[None], axis=1), jnp.sum(s * s, axis=1)]
        y = boxes(jnp.stack(kinds, axis=1).reshape(count * 24, 128)).reshape(count, 3, 8, 128)
        z = y[:, 0] * masks[0][None] + y[:, 1] * masks[1][None] + y[:, 2] * masks[2][None]
        means.append(jnp.sum(z, axis=1))
    z = jnp.concatenate(means, axis=0)
    q = jnp.where(iota((64, 128), 1) < 64, pltpu.roll(z, 64, 1), 1.0)
    c = z * (8.0 / jnp.sqrt((power + 1e-06) * (q + 1e-06)))
    c_hi, c_lo = split(c)
    out = dot(filt, jnp.concatenate([c_hi, c_hi, c_lo, c_lo], axis=0)).T
    out_ref[0] = out[:32]
    out_ref[1] = out[32:64]

    @pl.loop(0, n)
    def _(k):
        @pl.when(k != me)
        def _():
            block_copy(me, k).wait_send()


def shards(primary, secondaries, shift_az, shift_rg, frac_index):
    n = NB
    hbm = pl.BlockSpec(memory_space=pl.ANY)
    out = pl.pallas_call(
        kernel,
        out_shape=jax.ShapeDtypeStruct((2, 32, 64), F32),
        in_specs=[hbm] * 5,
        out_specs=pl.BlockSpec(memory_space=pltpu.VMEM),
        scratch_shapes=[
            pltpu.SMEM((2,), jnp.int32),
            pltpu.SMEM((2,), jnp.int32),
            pltpu.SMEM((2, 2), jnp.int32),
            pltpu.VMEM((32, 128), BF16),
            pltpu.VMEM((128, WIDTH), BF16),
            pltpu.VMEM((2, 64, WIDTH), BF16),
            pltpu.VMEM((n, 64, 128), BF16),
            pltpu.VMEM((n, 64, 128), BF16),
            pltpu.SemaphoreType.DMA((8,)),
            pltpu.SemaphoreType.DMA((n,)),
            pltpu.SemaphoreType.DMA((n,)),
            pltpu.SemaphoreType.REGULAR((4,)),
            pltpu.SemaphoreType.REGULAR,
        ],
        compiler_params=pltpu.CompilerParams(
            collective_id=0, has_side_effects=True, vmem_limit_bytes=64 * 2**20
        ),
    )(shift_az, shift_rg, frac_index, primary.reshape(32, 128), secondaries.reshape(128, WIDTH))
    return jnp.transpose(out, (0, 2, 1))


def solution(mesh):
    in_specs = (
        P("tile", None, "date"),
        P("date", "tile", None, None),
        P(("tile", "date")),
        P(("tile", "date")),
        P("date", "tile"),
    )
    out_specs = P("tile", None, "date")
    return jax.shard_map(shards, mesh=mesh, in_specs=in_specs, out_specs=out_specs, check_vma=False)
```

time: 35.2 us -> 29.2 us (0.83)
  Pallas kernels: 33.6 us -> 27.6 us
    pallas_call x1, Pallas kernels: 33.6 us -> 27.6 us  [shards(): pl.pallas_call(kernel, out_shape=jax.ShapeDtypeStruct((2, 32, 64), F32),...]
where the time goes in v2:
time: 29.2 us; the launch traced here: 29 us
  Pallas kernels  27.6 us (95%)
  local copies, waits for them, and re-layouts  1.38 us (5%)
    pallas_call x1, Pallas kernels, shards(): pl.pallas_call(kernel, out_shape=jax.ShapeDtypeStruct((2, 32, 64), F32),...  27.6 us
    unnamed x1, local copies, waits for them, and re-layouts  1.38 us

profile of v2, /device:TPU:1, one launch (start us, length us, event | category | flops | bytes accessed | tf_op | source)
XLA Modules:
  0.0 29.0 jit_solution(5951227026302205479)
XLA Ops:
  0.0 27.6 %shard_map.55 = f32[2,32,64]{2,1,0:T(8,128)} custom-call(s32[2]{0:T(128)} %saz_ref.1, s32[2]{0:T(128)} %srg_ref.1, s32[2,2]{1,0:T(2,128)} %frac_ref.1, bf16[32,128]{1,0:T(8,128)(2,1)} %bitcast.5, bf16[128,4224]{1,0:T(8,128)(2,1)} %bitcast.3), custom_call_target="tpu_custom_call" | custom-call | tf_op jit(solution)/shard_map/pallas_call | solution.py:237
  27.6 1.4 %copy.7 = f32[2,64,32]{1,2,0:T(8,128)} copy(f32[2,64,32]{1,2,0:T(8,128)} %bitcast.4) | data formatting | bytes 32768

commit v3 on v2

v3 whole, which is shorter than its diff:
```python
import jax
import jax.numpy as jnp
import numpy as np
from jax import lax
from jax.experimental import pallas as pl
from jax.experimental.pallas import tpu as pltpu
from jax.sharding import PartitionSpec as P

F32 = jnp.float32
BF16 = jnp.bfloat16
WIDTH = 4224
BLOCK = 128
NB = 32
HALF = NB // 2
PIECES = (0, 9, 17, 25, 33)
MESH = pl.DeviceIdType.MESH


def iota(shape, dim):
    return lax.broadcasted_iota(jnp.int32, shape, dim)


def split(x):
    hi = x.astype(BF16)
    return hi, (x - hi.astype(F32)).astype(BF16)


def dot(a, b):
    return jnp.dot(a, b, preferred_element_type=F32)


def tap_table():
    t = np.arange(8)[None] - 3.0 - np.arange(64)[:, None] / 64.0
    return (np.sinc(t) * (0.5 + 0.5 * np.cos(np.pi * t / 4.0))).astype(np.float32).reshape(-1)


def azimuth_matrix(a, taps):
    row, col = iota((32, 128), 0), iota((32, 128), 1)
    line = (row % 4) * 4 + row // 8
    same = (row // 4) % 2 == (col // 32) % 2
    dates = []
    for d in range(2):
        u = col % 32 - line - a[d]
        u = jnp.where(same & (col // 64 == d), u, -1)
        out = jnp.zeros((32, 128), F32)
        for j in range(8):
            out = jnp.where(u == j, taps[d][j], out)
        dates.append(out)
    return jnp.concatenate(dates, axis=0)


def range_matrix(r, taps):
    u = (iota((8, 128), 0) - iota((8, 128), 1) - r + 256) % 128
    rows = jnp.zeros((8, 128), F32)
    for j in range(8):
        rows = jnp.where(u == j, taps[j], rows)
    turned = [rows] + [pltpu.roll(rows, 8 * k, 1) for k in range(1, 16)]
    u = iota((256, 128), 0) - iota((256, 128), 1) - r
    return jnp.where((u >= 0) & (u < 8), jnp.concatenate(turned * 2, axis=0), 0.0)


def kernel(
    saz_ref, srg_ref, frac_ref, table_ref, prim_ref, sec_ref, out_ref,
    saz, srg, frac, table, prim, slab, along, tx, rx, in_sem, send_sem, recv_sem, late_sem, go_sem, turn_sem,
):
    n = NB
    me = lax.axis_index("date")
    early = me < HALF

    small = [
        pltpu.make_async_copy(src, dst, in_sem.at[k])
        for k, (src, dst) in enumerate(((saz_ref, saz), (srg_ref, srg), (frac_ref, frac), (table_ref, table), (prim_ref, prim)))
    ]

    def piece(c):
        return pl.ds(PIECES[c] * BLOCK, (PIECES[c + 1] - PIECES[c]) * BLOCK)

    def load(c):
        return pltpu.make_async_copy(sec_ref.at[:, piece(c)], slab.at[:, piece(c)], in_sem.at[5 + c])

    barrier = pltpu.get_barrier_semaphore()

    @pl.when(early)
    def _():
        for k in range(n - 1, HALF - 1, -1):
            pl.semaphore_signal(barrier, inc=1, device_id={"date": k}, device_id_type=MESH)

        @pl.loop(0, HALF)
        def _(k):
            @pl.when(k != me)
            def _():
                pl.semaphore_signal(barrier, inc=1, device_id={"date": k}, device_id_type=MESH)

    for copy in small:
        copy.start()
    for c in range(4):
        load(c).start()

    for copy in small[:4]:
        copy.wait()
    taps = [[[table[frac[d, x] * 8 + j] for j in range(8)] for x in range(2)] for d in range(2)]
    a_hi, a_lo = split(azimuth_matrix((saz[0], saz[1]), (taps[0][0], taps[1][0])))
    a_both = jnp.concatenate([a_hi, a_lo], axis=0)
    b_both = []
    for d in range(2):
        b_hi, b_lo = split(range_matrix(srg[d], taps[d][1]))
        b_both.append(jnp.concatenate([b_hi, b_lo], axis=1))

    def resample(c):
        load(c).wait()
        y = dot(a_both, slab[:, piece(c)])
        hi, lo = split(y[:64] + y[64:])
        for d in range(2):
            along[d, :32, piece(c)] = hi[32 * d : 32 * d + 32]
            along[d, 32:, piece(c)] = lo[32 * d : 32 * d + 32]
        first = 8 * c
        for d in range(2):
            whole = along[d, :, pl.ds(first * BLOCK, 9 * BLOCK)]
            rows = jnp.concatenate([whole[:, BLOCK * b : BLOCK * b + 256] for b in range(8)], axis=0)
            y = dot(rows, b_both[d]).reshape(8, 64, 256)
            full = y[:, :32, :128] + (y[:, :32, 128:] + y[:, 32:, :128])
            tx[pl.ds(first, 8), pl.ds(32 * d, 32)] = full.astype(BF16)

    def block_copy(src, dst):
        return pltpu.make_async_remote_copy(
            src_ref=tx.at[dst], dst_ref=rx.at[src], send_sem=send_sem.at[dst], recv_sem=recv_sem.at[src],
            device_id={"date": dst}, device_id_type=MESH,
        )

    def send(lo, hi):
        @pl.loop(lo, hi)
        def _(k):
            @pl.when(k != me)
            def _():
                block_copy(me, k).start()

    def sent(lo, hi):
        @pl.loop(lo, hi)
        def _(k):
            @pl.when(k != me)
            def _():
                block_copy(me, k).wait_send()

    plane = me // 4
    late = jnp.logical_not(early)

    @pl.when(early)
    def _():
        pl.semaphore_wait(barrier, HALF - 1)

    @pl.when(late)
    def _():
        pl.semaphore_wait(barrier, HALF)
        for k in range(HALF):
            pl.semaphore_signal(late_sem.at[plane - 4], inc=1, device_id={"date": k}, device_id_type=MESH)

    resample(0)
    send(0, 8)
    resample(1)

    send(8, 16)

    resample(2)
    resample(3)
    rx[me] = tx[me]

    small[4].wait()
    row, col = iota((32, 32), 0), iota((32, 32), 1)
    want = ((row // 4) % 2) * 16 + (row % 4) * 4 + row // 8
    order = jnp.where(col == want, 1.0, 0.0).astype(BF16)
    p = dot(order, prim[...]).reshape(4, 8, 128)
    swapped = jnp.concatenate([p[:, 4:], p[:, :4]], axis=1)

    look = (iota((256, 128), 0) % 128) // 16
    box = jnp.where(look == (iota((256, 128), 1) % 32) // 4, 1.0, 0.0).astype(BF16)
    sub, lane = iota((8, 128), 0), iota((8, 128), 1)
    hit = jnp.where(sub % 4 == lane % 4, 1.0 / 64.0, 0.0)
    part = lane // 32
    masks = (
        jnp.where(part == 0, hit, 0.0),
        jnp.where(part == 1, jnp.where(sub < 4, -hit, hit), 0.0),
        jnp.where(part >= 2, hit, 0.0),
    )

    def boxes(x):
        hi, lo = split(x)
        return dot(jnp.concatenate([hi, lo], axis=1), box)

    power = jnp.sum(boxes(jnp.sum(p * p, axis=0)) * hit, axis=0, keepdims=True)

    row, col = iota((64, 256), 0), iota((64, 256), 1)
    gap = (row - col % 64).astype(F32)
    w = jnp.exp(-(gap * gap) / 128.0)
    total = jnp.sum(jnp.where(col < 64, w, 0.0), axis=1, keepdims=True)
    high = jnp.where(gap == 0.0, 1.0, 0.0) - w / total
    h_hi, h_lo = split(high)
    filt = jnp.where((col // 64) % 2 == 0, h_hi.astype(F32), h_lo.astype(F32)).astype(BF16)

    @pl.when(late)
    def _():
        pl.semaphore_wait(go_sem, 1)
        send(HALF, n)

    @pl.when(early)
    def _():
        @pl.loop(0, 4)
        def _(to):
            pl.semaphore_wait(late_sem.at[to], 4)

            @pl.when((plane == 0) | ((plane == 1) & (to < 2)) | ((plane == 2) & (to < 2)) | ((plane == 3) & (to < 3)))
            def _():
                send(HALF + 4 * to, HALF + 4 * to + 4)

    @pl.when((plane == 0) | (plane == 3))
    def _():
        first = HALF + me % 4 + 8 * (1 - plane // 3)
        pl.semaphore_signal(go_sem, inc=1, device_id={"date": first}, device_id_type=MESH)
        pl.semaphore_signal(go_sem, inc=1, device_id={"date": first + 4}, device_id_type=MESH)

    def turn():
        @pl.when(plane == 0)
        def _():
            sent(16, 20)

            @pl.loop(1, 4)
            def _(k):
                pl.semaphore_signal(turn_sem, inc=1, device_id={"date": me + 4 * k}, device_id_type=MESH)

        @pl.when(early & (plane > 0))
        def _():
            pl.semaphore_wait(turn_sem, 1)

        @pl.when(plane == 1)
        def _():
            send(24, n)

        @pl.when(plane == 2)
        def _():
            send(24, n)

        @pl.when(plane == 3)
        def _():
            send(28, n)

    means = []
    for lo, hi in ((0, 16), (16, 24), (24, 32)):
        count = 2 * (hi - lo)

        @pl.loop(lo, hi)
        def _(k):
            @pl.when(k != me)
            def _():
                block_copy(k, k).wait_recv()

        s = rx[lo:hi].astype(F32).reshape(count, 4, 8, 128)
        kinds = [jnp.sum(s * p[None], axis=1), jnp.sum(s * swapped[None], axis=1), jnp.sum(s * s, axis=1)]
        y = boxes(jnp.stack(kinds, axis=1).reshape(count * 24, 128)).reshape(count, 3, 8, 128)
        z = y[:, 0] * masks[0][None] + y[:, 1] * masks[1][None] + y[:, 2] * masks[2][None]
        means.append(jnp.sum(z, axis=1))
        if lo == 0:
            turn()
    z = jnp.concatenate(means, axis=0)
    q = jnp.where(iota((64, 128), 1) < 64, pltpu.roll(z, 64, 1), 1.0)
    c = z * (8.0 / jnp.sqrt((power + 1e-06) * (q + 1e-06)))
    c_hi, c_lo = split(c)
    out = dot(filt, jnp.concatenate([c_hi, c_hi, c_lo, c_lo], axis=0)).T
    out_ref[0] = out[:32]
    out_ref[1] = out[32:64]

    sent(20, n)

    @pl.when(plane != 0)
    def _():
        sent(16, 20)

    sent(8, 16)

    sent(0, 8)


def shards(primary, secondaries, shift_az, shift_rg, frac_index):
    n = NB
    hbm = pl.BlockSpec(memory_space=pl.ANY)
    operands = (
        shift_az, shift_rg, frac_index, jnp.asarray(tap_table()), primary.reshape(32, 128), secondaries.reshape(128, WIDTH),
    )
    operands = [pltpu.with_memory_space_constraint(x, pltpu.HBM) for x in operands]
    out = pl.pallas_call(
        kernel,
        out_shape=pltpu.VMEM((2, 32, 64), F32),
        in_specs=[hbm] * 6,
        out_specs=pl.BlockSpec(memory_space=pltpu.VMEM),
        scratch_shapes=[
            pltpu.SMEM((2,), jnp.int32),
            pltpu.SMEM((2,), jnp.int32),
            pltpu.SMEM((2, 2), jnp.int32),
            pltpu.SMEM((512,), F32),
            pltpu.VMEM((32, 128), BF16),
            pltpu.VMEM((128, WIDTH), BF16),
            pltpu.VMEM((2, 64, WIDTH), BF16),
            pltpu.VMEM((n, 64, 128), BF16),
            pltpu.VMEM((n, 64, 128), BF16),
            pltpu.SemaphoreType.DMA((9,)),
            pltpu.SemaphoreType.DMA((n,)),
            pltpu.SemaphoreType.DMA((n,)),
            pltpu.SemaphoreType.REGULAR((4,)),
            pltpu.SemaphoreType.REGULAR,
            pltpu.SemaphoreType.REGULAR,
        ],
        compiler_params=pltpu.CompilerParams(
            collective_id=0, has_side_effects=True, vmem_limit_bytes=48 * 2**20
        ),
    )(*operands)
    return jnp.transpose(out, (0, 2, 1))


def solution(mesh):
    in_specs = (
        P("tile", None, "date"),
        P("date", "tile", None, None),
        P(("tile", "date")),
        P(("tile", "date")),
        P("date", "tile"),
    )
    out_specs = P("tile", None, "date")
    return jax.shard_map(shards, mesh=mesh, in_specs=in_specs, out_specs=out_specs, check_vma=False)
```

time: 29.2 us -> 25.7 us (0.88)
  the two profiles are of different devices: /device:TPU:1 before, /device:TPU:64 now
where the time goes in v3:
time: 25.7 us; the launch traced here: 25.5 us
  Pallas kernels  24.9 us (97%)
  local copies, waits for them, and re-layouts  0.62 us (2%)
    pallas_call x1, Pallas kernels, shards(): pl.pallas_call(kernel, out_shape=pltpu.VMEM((2, 32, 64), F32), in_specs=[...  24.9 us
    unnamed x1, local copies, waits for them, and re-layouts  0.62 us

profile of v3, /device:TPU:64, one launch (start us, length us, event | category | flops | bytes accessed | tf_op | source)
XLA Modules:
  0.0 25.5 jit_solution(800227005008616305)
XLA Ops:
  0.0 24.9 %shard_map.64 = f32[2,32,64]{2,1,0:T(8,128)S(1)} custom-call(s32[2]{0:T(128)} %saz_ref.1, s32[2]{0:T(128)} %srg_ref.1, s32[2,2]{1,0:T(2,128)} %frac_ref.1, f32[512]{0:T(512)} %constant.2.clone.table_ref, bf16[32,128]{1,0:T(8,128)(2,1)} %bitcast.5, bf16[128,4224]{1,0:T(8,128)(2,1)} %bitcast.4), custom_call_target="tpu_custom_call" | custom-call | tf_op jit(solution)/shard_map/pallas_call | solution.py:288
  24.9 0.6 %copy.8 = f32[2,64,32]{1,2,0:T(8,128)} copy(f32[2,64,32]{1,2,0:T(8,128)S(1)} %bitcast.3) | data formatting | bytes 32768

commit v4 on v3

--- a/solution.py
+++ b/solution.py
@@ -11,8 +11,10 @@
 WIDTH = 4224
 BLOCK = 128
 NB = 32
-HALF = NB // 2
-PIECES = (0, 9, 17, 25, 33)
+PLANES = 4
+FIRST_LATE = 4 * PLANES
+PIECES = (0, 5, 9, 17, 25, 33)
+FIRST = (0, 4, 8, 16, 24, 32)
 MESH = pl.DeviceIdType.MESH
 
 
@@ -61,11 +63,12 @@
 
 def kernel(
     saz_ref, srg_ref, frac_ref, table_ref, prim_ref, sec_ref, out_ref,
-    saz, srg, frac, table, prim, slab, along, tx, rx, in_sem, send_sem, recv_sem, late_sem, go_sem, turn_sem,
+    saz, srg, frac, table, prim, slab, along, tx, rx, z_ref, in_sem, send_sem, recv_sem, late_sem, go_sem, turn_sem,
 ):
     n = NB
     me = lax.axis_index("date")
-    early = me < HALF
+    plane = me // 4
+    early = me < FIRST_LATE
 
     small = [
         pltpu.make_async_copy(src, dst, in_sem.at[k])
@@ -82,10 +85,10 @@
 
     @pl.when(early)
     def _():
-        for k in range(n - 1, HALF - 1, -1):
+        for k in range(n - 1, FIRST_LATE - 1, -1):
             pl.semaphore_signal(barrier, inc=1, device_id={"date": k}, device_id_type=MESH)
 
-        @pl.loop(0, HALF)
+        @pl.loop(0, FIRST_LATE)
         def _(k):
             @pl.when(k != me)
             def _():
@@ -93,7 +96,7 @@
 
     for copy in small:
         copy.start()
-    for c in range(4):
+    for c in range(5):
         load(c).start()
 
     for copy in small[:4]:
@@ -113,19 +116,35 @@
         for d in range(2):
             along[d, :32, piece(c)] = hi[32 * d : 32 * d + 32]
             along[d, 32:, piece(c)] = lo[32 * d : 32 * d + 32]
-        first = 8 * c
+        first, many = FIRST[c], FIRST[c + 1] - FIRST[c]
         for d in range(2):
-            whole = along[d, :, pl.ds(first * BLOCK, 9 * BLOCK)]
-            rows = jnp.concatenate([whole[:, BLOCK * b : BLOCK * b + 256] for b in range(8)], axis=0)
-            y = dot(rows, b_both[d]).reshape(8, 64, 256)
+            whole = along[d, :, pl.ds(first * BLOCK, (many + 1) * BLOCK)]
+            rows = jnp.concatenate([whole[:, BLOCK * b : BLOCK * b + 256] for b in range(many)], axis=0)
+            y = dot(rows, b_both[d]).reshape(many, 64, 256)
             full = y[:, :32, :128] + (y[:, :32, 128:] + y[:, 32:, :128])
-            tx[pl.ds(first, 8), pl.ds(32 * d, 32)] = full.astype(BF16)
+            tx[pl.ds(first, many), pl.ds(32 * d, 32)] = full.astype(BF16)
+
+    def class_of(k):
+        return ((k + n - FIRST_LATE) // n) * (k // 4 - PLANES + 1)
 
     def block_copy(src, dst):
         return pltpu.make_async_remote_copy(
-            src_ref=tx.at[dst], dst_ref=rx.at[src], send_sem=send_sem.at[dst], recv_sem=recv_sem.at[src],
+            src_ref=tx.at[dst], dst_ref=rx.at[src],
+            send_sem=send_sem.at[class_of(dst)], recv_sem=recv_sem.at[class_of(src)],
             device_id={"date": dst}, device_id_type=MESH,
         )
+
+    def wait_class(c, full, mine, received):
+        for count, here in ((full - 1, mine), (full, jnp.logical_not(mine))):
+
+            @pl.when(here)
+            def _():
+                copy = pltpu.make_async_remote_copy(
+                    src_ref=tx.at[pl.ds(0, count)], dst_ref=rx.at[pl.ds(0, count)],
+                    send_sem=send_sem.at[c], recv_sem=recv_sem.at[c],
+                    device_id={"date": (me + 1) % n}, device_id_type=MESH,
+                )
+                copy.wait_recv() if received else copy.wait_send()
 
     def send(lo, hi):
         @pl.loop(lo, hi)
@@ -134,34 +153,26 @@
             def _():
                 block_copy(me, k).start()
 
-    def sent(lo, hi):
-        @pl.loop(lo, hi)
-        def _(k):
-            @pl.when(k != me)
-            def _():
-                block_copy(me, k).wait_send()
-
-    plane = me // 4
     late = jnp.logical_not(early)
 
     @pl.when(early)
     def _():
-        pl.semaphore_wait(barrier, HALF - 1)
+        pl.semaphore_wait(barrier, FIRST_LATE - 1)
 
     @pl.when(late)
     def _():
-        pl.semaphore_wait(barrier, HALF)
-        for k in range(HALF):
-            pl.semaphore_signal(late_sem.at[plane - 4], inc=1, device_id={"date": k}, device_id_type=MESH)
+        pl.semaphore_wait(barrier, FIRST_LATE)
+        for k in range(FIRST_LATE):
+            pl.semaphore_signal(late_sem.at[plane - PLANES], inc=1, device_id={"date": k}, device_id_type=MESH)
 
     resample(0)
-    send(0, 8)
+    send(0, 4)
     resample(1)
-
-    send(8, 16)
-
+    send(4, 8)
     resample(2)
+    send(8, FIRST_LATE)
     resample(3)
+    resample(4)
     rx[me] = tx[me]
 
     small[4].wait()
@@ -199,30 +210,37 @@
     @pl.when(late)
     def _():
         pl.semaphore_wait(go_sem, 1)
-        send(HALF, n)
+        send(FIRST_LATE, n)
+
+    def held(to):
+        return ((plane == 1) & (to >= 6)) | ((plane == 2) & (to >= 6)) | ((plane == 3) & (to >= 7))
 
     @pl.when(early)
     def _():
-        @pl.loop(0, 4)
+        @pl.loop(PLANES, 8)
         def _(to):
-            pl.semaphore_wait(late_sem.at[to], 4)
-
-            @pl.when((plane == 0) | ((plane == 1) & (to < 2)) | ((plane == 2) & (to < 2)) | ((plane == 3) & (to < 3)))
+            pl.semaphore_wait(late_sem.at[to - PLANES], 4)
+
+            @pl.when(jnp.logical_not(held(to)))
             def _():
-                send(HALF + 4 * to, HALF + 4 * to + 4)
-
-    @pl.when((plane == 0) | (plane == 3))
-    def _():
-        first = HALF + me % 4 + 8 * (1 - plane // 3)
-        pl.semaphore_signal(go_sem, inc=1, device_id={"date": first}, device_id_type=MESH)
-        pl.semaphore_signal(go_sem, inc=1, device_id={"date": first + 4}, device_id_type=MESH)
+                send(4 * to, 4 * to + 4)
+
+    @pl.when(plane == 0)
+    def _():
+        for to in (6, 7):
+            pl.semaphore_signal(go_sem, inc=1, device_id={"date": me % 4 + 4 * to}, device_id_type=MESH)
+
+    @pl.when(plane == 3)
+    def _():
+        for to in (4, 5):
+            pl.semaphore_signal(go_sem, inc=1, device_id={"date": me % 4 + 4 * to}, device_id_type=MESH)
 
     def turn():
         @pl.when(plane == 0)
         def _():
-            sent(16, 20)
-
-            @pl.loop(1, 4)
+            wait_class(1, 4, plane == 4, False)
+
+            @pl.loop(1, PLANES)
             def _(k):
                 pl.semaphore_signal(turn_sem, inc=1, device_id={"date": me + 4 * k}, device_id_type=MESH)
 
@@ -230,36 +248,32 @@
         def _():
             pl.semaphore_wait(turn_sem, 1)
 
-        @pl.when(plane == 1)
-        def _():
-            send(24, n)
-
-        @pl.when(plane == 2)
-        def _():
-            send(24, n)
-
-        @pl.when(plane == 3)
-        def _():
-            send(28, n)
-
-    means = []
-    for lo, hi in ((0, 16), (16, 24), (24, 32)):
-        count = 2 * (hi - lo)
-
-        @pl.loop(lo, hi)
-        def _(k):
-            @pl.when(k != me)
-            def _():
-                block_copy(k, k).wait_recv()
-
-        s = rx[lo:hi].astype(F32).reshape(count, 4, 8, 128)
+            @pl.loop(PLANES, 8)
+            def _(to):
+                @pl.when(held(to))
+                def _():
+                    send(4 * to, 4 * to + 4)
+
+    def process(rows):
+        count = 2 * rows.shape[0]
+        s = rows.astype(F32).reshape(count, 4, 8, 128)
         kinds = [jnp.sum(s * p[None], axis=1), jnp.sum(s * swapped[None], axis=1), jnp.sum(s * s, axis=1)]
         y = boxes(jnp.stack(kinds, axis=1).reshape(count * 24, 128)).reshape(count, 3, 8, 128)
         z = y[:, 0] * masks[0][None] + y[:, 1] * masks[1][None] + y[:, 2] * masks[2][None]
-        means.append(jnp.sum(z, axis=1))
-        if lo == 0:
-            turn()
-    z = jnp.concatenate(means, axis=0)
+        return jnp.sum(z, axis=1)
+
+    wait_class(0, FIRST_LATE, early, False)
+    wait_class(0, FIRST_LATE, early, True)
+    z_ref[pl.ds(0, 2 * FIRST_LATE)] = process(rx[:FIRST_LATE])
+    turn()
+    wait_class(1, 4, plane == 4, True)
+    wait_class(2, 4, plane == 5, True)
+    z_ref[pl.ds(32, 16)] = process(rx[16:24])
+    wait_class(3, 4, plane == 6, True)
+    wait_class(4, 4, plane == 7, True)
+    z_ref[pl.ds(48, 16)] = process(rx[24:32])
+
+    z = z_ref[...]
     q = jnp.where(iota((64, 128), 1) < 64, pltpu.roll(z, 64, 1), 1.0)
     c = z * (8.0 / jnp.sqrt((power + 1e-06) * (q + 1e-06)))
     c_hi, c_lo = split(c)
@@ -267,15 +281,13 @@
     out_ref[0] = out[:32]
     out_ref[1] = out[32:64]
 
-    sent(20, n)
+    for to in range(PLANES, 8):
+        if to != 4:
+            wait_class(to - PLANES + 1, 4, plane == to, False)
 
     @pl.when(plane != 0)
     def _():
-        sent(16, 20)
-
-    sent(8, 16)
-
-    sent(0, 8)
+        wait_class(1, 4, plane == 4, False)
 
 
 def shards(primary, secondaries, shift_az, shift_rg, frac_index):
@@ -300,10 +312,11 @@
             pltpu.VMEM((2, 64, WIDTH), BF16),
             pltpu.VMEM((n, 64, 128), BF16),
             pltpu.VMEM((n, 64, 128), BF16),
-            pltpu.SemaphoreType.DMA((9,)),
-            pltpu.SemaphoreType.DMA((n,)),
-            pltpu.SemaphoreType.DMA((n,)),
-            pltpu.SemaphoreType.REGULAR((4,)),
+            pltpu.VMEM((64, 128), F32),
+            pltpu.SemaphoreType.DMA((10,)),
+            pltpu.SemaphoreType.DMA((9 - PLANES,)),
+            pltpu.SemaphoreType.DMA((9 - PLANES,)),
+            pltpu.SemaphoreType.REGULAR((8 - PLANES,)),
             pltpu.SemaphoreType.REGULAR,
             pltpu.SemaphoreType.REGULAR,
         ],

time: 25.7 us -> 25.2 us (0.981)
  Pallas kernels: 24.9 us -> 24.3 us
    pallas_call x1, Pallas kernels: 24.9 us -> 24.3 us  [shards(): pl.pallas_call(kernel, out_shape=pltpu.VMEM((2, 32, 64), F32), in_specs=[...]
where the time goes in v4:
time: 25.2 us; the launch traced here: 25 us
  Pallas kernels  24.3 us (96%)
  local copies, waits for them, and re-layouts  0.62 us (2%)
    pallas_call x1, Pallas kernels, shards(): pl.pallas_call(kernel, out_shape=pltpu.VMEM((2, 32, 64), F32), in_specs=[...  24.3 us
    unnamed x1, local copies, waits for them, and re-layouts  0.62 us

profile of v4, /device:TPU:64, one launch (start us, length us, event | category | flops | bytes accessed | tf_op | source)
XLA Modules:
  0.0 25.0 jit_solution(11932791140353054256)
XLA Ops:
  0.0 24.3 %shard_map.64 = f32[2,32,64]{2,1,0:T(8,128)S(1)} custom-call(s32[2]{0:T(128)} %saz_ref.1, s32[2]{0:T(128)} %srg_ref.1, s32[2,2]{1,0:T(2,128)} %frac_ref.1, f32[512]{0:T(512)} %constant.2.clone.table_ref, bf16[32,128]{1,0:T(8,128)(2,1)} %bitcast.5, bf16[128,4224]{1,0:T(8,128)(2,1)} %bitcast.4), custom_call_target="tpu_custom_call" | custom-call | tf_op jit(solution)/shard_map/pallas_call | solution.py:300
  24.4 0.6 %copy.8 = f32[2,64,32]{1,2,0:T(8,128)} copy(f32[2,64,32]{1,2,0:T(8,128)S(1)} %bitcast.3) | data formatting | bytes 32768

commit v5 on v4

--- a/solution.py
+++ b/solution.py
@@ -238,7 +238,7 @@
     def turn():
         @pl.when(plane == 0)
         def _():
-            wait_class(1, 4, plane == 4, False)
+            wait_class(2, 4, plane == 5, False)
 
             @pl.loop(1, PLANES)
             def _(k):
@@ -282,12 +282,12 @@
     out_ref[1] = out[32:64]
 
     for to in range(PLANES, 8):
-        if to != 4:
+        if to != 5:
             wait_class(to - PLANES + 1, 4, plane == to, False)
 
     @pl.when(plane != 0)
     def _():
-        wait_class(1, 4, plane == 4, False)
+        wait_class(2, 4, plane == 5, False)
 
 
 def shards(primary, secondaries, shift_az, shift_rg, frac_index):

time: 25.2 us -> 25.1 us (level)
  no operation moved by 1% of the time
where the time goes in v5:
time: 25.1 us; the launch traced here: 25 us
  Pallas kernels  24.3 us (97%)
  local copies, waits for them, and re-layouts  0.62 us (2%)
    pallas_call x1, Pallas kernels, shards(): pl.pallas_call(kernel, out_shape=pltpu.VMEM((2, 32, 64), F32), in_specs=[...  24.3 us
    unnamed x1, local copies, waits for them, and re-layouts  0.62 us

profile of v5, /device:TPU:64, one launch (start us, length us, event | category | flops | bytes accessed | tf_op | source)
XLA Modules:
  0.0 25.0 jit_solution(12498760789186239209)
XLA Ops:
  0.0 24.3 %shard_map.64 = f32[2,32,64]{2,1,0:T(8,128)S(1)} custom-call(s32[2]{0:T(128)} %saz_ref.1, s32[2]{0:T(128)} %srg_ref.1, s32[2,2]{1,0:T(2,128)} %frac_ref.1, f32[512]{0:T(512)} %constant.2.clone.table_ref, bf16[32,128]{1,0:T(8,128)(2,1)} %bitcast.5, bf16[128,4224]{1,0:T(8,128)(2,1)} %bitcast.4), custom_call_target="tpu_custom_call" | custom-call | tf_op jit(solution)/shard_map/pallas_call | solution.py:300
  24.4 0.6 %copy.8 = f32[2,64,32]{1,2,0:T(8,128)} copy(f32[2,64,32]{1,2,0:T(8,128)S(1)} %bitcast.3) | data formatting | bytes 32768

commit v6 on v5

--- a/solution.py
+++ b/solution.py
@@ -213,7 +213,7 @@
         send(FIRST_LATE, n)
 
     def held(to):
-        return ((plane == 1) & (to >= 6)) | ((plane == 2) & (to >= 6)) | ((plane == 3) & (to >= 7))
+        return ((plane > 0) & (to >= 7)) | ((plane == 1) & (to >= 6))
 
     @pl.when(early)
     def _():

time: 25.1 us -> 25.1 us (level)
  no operation moved by 1% of the time
where the time goes in v6:
time: 25.1 us; the launch traced here: 25 us
  Pallas kernels  24.3 us (97%)
  local copies, waits for them, and re-layouts  0.62 us (2%)
    pallas_call x1, Pallas kernels, shards(): pl.pallas_call(kernel, out_shape=pltpu.VMEM((2, 32, 64), F32), in_specs=[...  24.3 us
    unnamed x1, local copies, waits for them, and re-layouts  0.62 us

profile of v6, /device:TPU:64, one launch (start us, length us, event | category | flops | bytes accessed | tf_op | source)
XLA Modules:
  0.0 25.0 jit_solution(5221498178003197308)
XLA Ops:
  0.0 24.3 %shard_map.64 = f32[2,32,64]{2,1,0:T(8,128)S(1)} custom-call(s32[2]{0:T(128)} %saz_ref.1, s32[2]{0:T(128)} %srg_ref.1, s32[2,2]{1,0:T(2,128)} %frac_ref.1, f32[512]{0:T(512)} %constant.2.clone.table_ref, bf16[32,128]{1,0:T(8,128)(2,1)} %bitcast.5, bf16[128,4224]{1,0:T(8,128)(2,1)} %bitcast.4), custom_call_target="tpu_custom_call" | custom-call | tf_op jit(solution)/shard_map/pallas_call | solution.py:300
  24.3 0.6 %copy.8 = f32[2,64,32]{1,2,0:T(8,128)} copy(f32[2,64,32]{1,2,0:T(8,128)S(1)} %bitcast.3) | data formatting | bytes 32768

commit v7 on v5

--- a/solution.py
+++ b/solution.py
@@ -270,8 +270,9 @@
     wait_class(2, 4, plane == 5, True)
     z_ref[pl.ds(32, 16)] = process(rx[16:24])
     wait_class(3, 4, plane == 6, True)
+    z_ref[pl.ds(48, 8)] = process(rx[24:28])
     wait_class(4, 4, plane == 7, True)
-    z_ref[pl.ds(48, 16)] = process(rx[24:32])
+    z_ref[pl.ds(56, 8)] = process(rx[28:32])
 
     z = z_ref[...]
     q = jnp.where(iota((64, 128), 1) < 64, pltpu.roll(z, 64, 1), 1.0)

time: 25.1 us -> 25.1 us (level)
  no operation moved by 1% of the time
where the time goes in v7:
time: 25.1 us; the launch traced here: 25 us
  Pallas kernels  24.3 us (97%)
  local copies, waits for them, and re-layouts  0.62 us (2%)
    pallas_call x1, Pallas kernels, shards(): pl.pallas_call(kernel, out_shape=pltpu.VMEM((2, 32, 64), F32), in_specs=[...  24.3 us
    unnamed x1, local copies, waits for them, and re-layouts  0.62 us

profile of v7, /device:TPU:64, one launch (start us, length us, event | category | flops | bytes accessed | tf_op | source)
XLA Modules:
  0.0 25.0 jit_solution(995546833145266531)
XLA Ops:
  0.0 24.3 %shard_map.64 = f32[2,32,64]{2,1,0:T(8,128)S(1)} custom-call(s32[2]{0:T(128)} %saz_ref.1, s32[2]{0:T(128)} %srg_ref.1, s32[2,2]{1,0:T(2,128)} %frac_ref.1, f32[512]{0:T(512)} %constant.2.clone.table_ref, bf16[32,128]{1,0:T(8,128)(2,1)} %bitcast.5, bf16[128,4224]{1,0:T(8,128)(2,1)} %bitcast.4), custom_call_target="tpu_custom_call" | custom-call | tf_op jit(solution)/shard_map/pallas_call | solution.py:301
  24.4 0.6 %copy.8 = f32[2,64,32]{1,2,0:T(8,128)} copy(f32[2,64,32]{1,2,0:T(8,128)S(1)} %bitcast.3) | data formatting | bytes 32768
